TPU v7x, 32 devices: a whole 2x2x4 slice. The times are simulated.
32 devices in a mesh: groups: 2 (over x), ctx: 8 (over z, y), rep: 2 (over core).
Axes of the slice: x: 2, y: 2, z: 4, core: 2. Of those that a mesh axis runs over, the one named last changes fastest.
Arguments:
- queries: bfloat16 [256, 16, 128], P(('groups', 'ctx', 'rep')), parts along dimension 0, may hold values from -40 to 40
- cache: bfloat16 [2, 2, 65536, 128], P('rep', None, ('groups', 'ctx')), parts along dimension 2, may hold values from -4 to 4
- owner: int32 [16], P(('groups', 'ctx')), parts along dimension 0, may hold values from 0 to 1
- lengths: int32 [256], P(('groups', 'ctx', 'rep')), parts along dimension 0, may hold values from 2 to 32768, as said below
Outputs:
- attended: bfloat16 [256, 16, 128], P(('groups', 'ctx', 'rep')), parts along dimension 0
There are 2 independent parts, one for each index of `groups`. A program takes and returns all parts, laid end to end along the dimension named above; each array names one. Nothing has to cross between parts.
Inputs may be any that keep to these rules, and one draw needn't show every extreme that they name: `lengths`: some request in every draw uses the whole prefix.
All inputs are finite; a program needn't handle non-finite values.
Results may differ from a plain program's by a relative error of at most 0.003.
Values may be sent and summed in bfloat16 or wider, within the bound.
A program may use at most 64 MiB of HBM per device.

v0:
```python
import math

import jax
import jax.numpy as jnp
from jax import lax
from jax.sharding import PartitionSpec as P


def from_root(array, axis, root):
    mine = lax.axis_index(axis) == root
    return lax.psum(jnp.where(mine, array, jnp.zeros_like(array)), axis)


def shard_partials(query_rows, row_lens, keys, values, start):
    scores = lax.dot_general(
        query_rows, keys, (((1,), (1,)), ((), ())), preferred_element_type=jnp.float32
    )
    scores = scores * keys.shape[1] ** (-0.5)
    positions = start + jnp.arange(keys.shape[0], dtype=jnp.int32)
    valid = positions[None, :] < row_lens[:, None]
    masked = jnp.where(valid, scores, jnp.float32(-1e30))
    top = jnp.max(masked, axis=1)
    weights = jnp.where(valid, jnp.exp(masked - top[:, None]), jnp.float32(0.0)).astype(
        jnp.bfloat16
    )
    total = jnp.sum(weights.astype(jnp.float32), axis=1)
    partial_value = jnp.dot(weights, values, preferred_element_type=jnp.float32)
    return (top, total, partial_value)


def per_device(queries, cache, owner, lengths):
    count = lax.axis_size("ctx")
    place = lax.axis_index("ctx")
    req, heads, width = queries.shape
    span = cache.shape[2]
    rows = req * heads
    shard_kv = from_root(cache[0], "rep", owner[0])
    keys = shard_kv[0]
    values = shard_kv[1]
    every_len = lax.all_gather(lengths, "ctx", axis=0, tiled=True)
    every_row_len = jnp.repeat(every_len, heads)
    query_rows = queries.reshape(rows, width)
    start = place * span
    every_query = lax.all_gather(query_rows, "ctx", axis=0, tiled=True)
    group = math.gcd(count, max(1, 512 // rows))
    query_blocks = every_query.reshape(count // group, group * rows, width)
    len_blocks = every_row_len.reshape(count // group, group * rows)

    def per_block(pair):
        return shard_partials(pair[0], pair[1], keys, values, start)

    tops, totals, partials = lax.map(per_block, (query_blocks, len_blocks))
    tops = tops.reshape(count * rows)
    totals = totals.reshape(count * rows)
    partials = partials.reshape(count * rows, width)
    tops, totals, partials = (
        lax.all_to_all(tops, "ctx", split_axis=0, concat_axis=0, tiled=True),
        lax.all_to_all(totals, "ctx", split_axis=0, concat_axis=0, tiled=True),
        lax.all_to_all(partials, "ctx", split_axis=0, concat_axis=0, tiled=True),
    )
    tops = tops.reshape(count, rows)
    totals = totals.reshape(count, rows)
    partials = partials.reshape(count, rows, width)
    top = jnp.max(tops, axis=0)
    scales = jnp.exp(tops - top[None, :])
    total = jnp.sum(scales * totals, axis=0)
    partial_value = jnp.sum(scales[:, :, None] * partials, axis=0)
    return (partial_value / total[:, None]).astype(jnp.bfloat16).reshape(req, heads, width)


def solution(mesh):
    placed = (
        P(("groups", "ctx", "rep"), None, None),
        P("rep", None, ("groups", "ctx"), None),
        P(("groups", "ctx")),
        P(("groups", "ctx", "rep")),
    )
    return jax.shard_map(
        per_device,
        mesh=mesh,
        in_specs=placed,
        out_specs=P(("groups", "ctx", "rep"), None, None),
        check_vma=False,
    )
```

profile of v0, /device:TPU:0, one launch (start us, length us, event | category | flops | bytes accessed | tf_op | source)
XLA Modules:
  0.0 112.6 jit_solution(7608086093900528834)
XLA Ops:
  7.2 3.0 %select_bitcast_fusion = bf16[2,4096,128]{2,1,0:T(8,128)(2,1)} fusion(bf16[1,2,4096,128]{3,2,1,0:T(8,128)(2,1)} %param.7, pred[]{:T(512)S(6)} %eq.3), kind=kLoop, calls=%fused_computation.13 | loop fusion | flops 1048576 | bytes 4194305 | tf_op jit(solution)/shard_map/jit(_where)/select_n | solution.py:11
  10.3 1.2 %dynamic-slice = u32[1]{0:T(128)} dynamic-slice(u32[32]{0:T(128)} %constant.48, u32[]{:T(128)S(6)} %add.15), dynamic_slice_sizes={1} | dynamic-slice | bytes 12
  12.1 0.9 dynamic-update-slice
  12.9 13.1 %all-reduce = s32[64]{0:T(128)S(1)} all-reduce(s32[64]{0:T(128)S(1)} %dynamic-update-slice), channel_id=1, replica_groups=mesh['groups'=2,'ctx'=8,'rep'=2] {'ctx'}, use_global_device_ids=true, to_apply=%add | all-reduce | flops 64 | bytes 512
  26.0 0.1 broadcast_in_dim.38
  26.1 0.1 broadcast_in_dim.40
  26.2 31.1 %all_gather.7 = bf16[1024,128]{1,0:T(8,128)(2,1)S(1)} all-gather(bf16[128,128]{1,0:T(8,128)(2,1)} %bitcast.54), channel_id=1, replica_groups=mesh['groups'=2,'ctx'=8,'rep'=2] {'ctx'}, dimensions={0}, use_global_device_ids=true | all-gather | bytes 294912 | tf_op jit(solution)/shard_map/all_gather | solution.py:44
  57.3 1.7 %slice_bitcast_fusion = (bf16[4096,128]{1,0:T(8,128)(2,1)S(1)}, bf16[4096,128]{1,0:T(8,128)(2,1)S(1)}) fusion(bf16[2,4096,128]{2,1,0:T(8,128)(2,1)} %all-reduce.3.cloned.1.call-done), kind=kLoop, calls=%fused_computation.14 | loop fusion | bytes 4194304 | tf_op jit(solution)/shard_map/squeeze | solution.py:39
  59.0 12.9 %while.14 = (s32[]{:T(128)}, f32[2,512]{1,0:T(2,128)S(1)}, f32[2,512]{1,0:T(2,128)S(1)}, f32[2,512,128]{2,1,0:T(8,128)}, s32[]{:T(128)}, /*index=5*/s32[2,512]{1...) while((s32[]{:T(128)}, f32[2,512]{1,0:T(2,128)S(1)}, ...), condition=%wide.region_4.5_spmd, body=%wide.region_1.4_spmd.sunk | while | flops 1098910720 | bytes 27728512 | solution.py:52
  59.0 1.7 %fusion.19 = (f32[512]{0:T(512)S(1)}, f32[512,4096]{1,0:T(8,128)S(1)}) fusion(s32[4096]{0:T(1024)S(1)} %iota_add_fusion.2, s32[512]{0:T(512)S(1)} %bitcast.51, bf16[4096,128]{1,0:T(8,128)(2,1)S(1)} %get-tuple-element.173, bf16[2,512,128]{2,1,0:T(8,128)(2,1)S(1)} %get-tuple-element.172, s32[]{:T(128)} %get-tuple-element.155), kind=kOutput, calls=%fused_computation.4.clone.1 | convolution fusion | flops 545259008 | bytes 9588740 | tf_op jit(solution)/shard_map/while/body/eval_jaxpr/dot_general | solution.py:15
  60.7 2.7 %convert_reduce_fusion.2 = (f32[512]{0:T(512)S(1)}, bf16[512,4096]{1,0:T(8,128)(2,1)S(1)}) fusion(f32[512]{0:T(512)S(1)} %get-tuple-element.140, f32[512,4096]{1,0:T(8,128)S(1)} %get-tuple-element.141, s32[512]{0:T(512)S(1)} %bitcast.52, s32[4096]{0:T(1024)S(1)} %iota_add_fusion.2), kind=kLoop, calls=%fused_computation.3.clone.1 | loop fusion | flops 16776704 | bytes 12605440 | tf_op jit(solution)/shard_map/while/body/eval_jaxpr/reduce_sum | solution.py:26
  63.4 1.9 %fusion.20 = f32[2,512,128]{2,1,0:T(8,128)} fusion(f32[2,512,128]{2,1,0:T(8,128)} %get-tuple-element.158, s32[]{:T(128)} %get-tuple-element.155, bf16[512,4096]{1,0:T(8,128)(2,1)S(1)} %get-tuple-element.143, bf16[4096,128]{1,0:T(8,128)(2,1)S(1)} %get-tuple-element.174), kind=kOutput, calls=%fused_computation.6.clone.1 | convolution fusion | flops 536870912 | bytes 5505536 | tf_op jit(solution)/shard_map/while/body/eval_jaxpr/dot_general | solution.py:27
  65.5 1.7 %fusion.19 = (f32[512]{0:T(512)S(1)}, f32[512,4096]{1,0:T(8,128)S(1)}) fusion(s32[4096]{0:T(1024)S(1)} %iota_add_fusion.2, s32[512]{0:T(512)S(1)} %bitcast.51, bf16[4096,128]{1,0:T(8,128)(2,1)S(1)} %get-tuple-element.173, bf16[2,512,128]{2,1,0:T(8,128)(2,1)S(1)} %get-tuple-element.172, s32[]{:T(128)} %get-tuple-element.155), kind=kOutput, calls=%fused_computation.4.clone.1 | convolution fusion | flops 545259008 | bytes 9588740 | tf_op jit(solution)/shard_map/while/body/eval_jaxpr/dot_general | solution.py:15
  67.1 2.7 %convert_reduce_fusion.2 = (f32[512]{0:T(512)S(1)}, bf16[512,4096]{1,0:T(8,128)(2,1)S(1)}) fusion(f32[512]{0:T(512)S(1)} %get-tuple-element.140, f32[512,4096]{1,0:T(8,128)S(1)} %get-tuple-element.141, s32[512]{0:T(512)S(1)} %bitcast.52, s32[4096]{0:T(1024)S(1)} %iota_add_fusion.2), kind=kLoop, calls=%fused_computation.3.clone.1 | loop fusion | flops 16776704 | bytes 12605440 | tf_op jit(solution)/shard_map/while/body/eval_jaxpr/reduce_sum | solution.py:26
  69.8 2.0 %fusion.20 = f32[2,512,128]{2,1,0:T(8,128)} fusion(f32[2,512,128]{2,1,0:T(8,128)} %get-tuple-element.158, s32[]{:T(128)} %get-tuple-element.155, bf16[512,4096]{1,0:T(8,128)(2,1)S(1)} %get-tuple-element.143, bf16[4096,128]{1,0:T(8,128)(2,1)S(1)} %get-tuple-element.174), kind=kOutput, calls=%fused_computation.6.clone.1 | convolution fusion | flops 536870912 | bytes 5505536 | tf_op jit(solution)/shard_map/while/body/eval_jaxpr/dot_general | solution.py:27
  71.9 0.6 all_to_all.18
  72.5 3.3 %all-to-all-start = ((f32[8,128,1]{1,2,0:T(1,128)}), f32[8,128,1]{1,2,0:T(1,128)S(1)}, u32[]{:S(2)}, u32[]{:S(2)}) async-start(f32[8,128,1]{1,2,0:T(1,128)} %all_to_all.18), calls=%async_computation | async-start | bytes 8192 | tf_op jit(solution)/shard_map/all_to_all | solution.py:57
  75.8 6.3 %all-to-all-done = f32[8,128,1]{1,2,0:T(1,128)S(1)} async-done(((f32[8,128,1]{1,2,0:T(1,128)}), f32[8,128,1]{1,2,0:T(1,128)S(1)}, u32[]{:S(2)}, u32[]{:S(2)}) %all-to-all-start) | async-done | bytes 4128 | tf_op jit(solution)/shard_map/all_to_all | solution.py:57
  82.1 9.0 %all_to_all.27 = f32[8,128,1]{1,2,0:T(1,128)S(1)} all-to-all(f32[8,128,1]{1,2,0:T(1,128)S(1)} %all_to_all.22), channel_id=1, replica_groups=mesh['groups'=2,'ctx'=8,'rep'=2] {'ctx'}, dimensions={0} | all-to-all | bytes 8192 | tf_op jit(solution)/shard_map/all_to_all | solution.py:58
  91.1 3.5 %all-to-all-start.1 = ((f32[8,128,128]{2,1,0:T(8,128)}), f32[8,128,128]{2,1,0:T(8,128)S(1)}, u32[]{:S(2)}, u32[]{:S(2)}) async-start(f32[8,128,128]{2,1,0:T(8,128)} %bitcast.13), calls=%async_computation.1 | async-start | bytes 1048576 | tf_op jit(solution)/shard_map/all_to_all | solution.py:59
  94.7 0.1 div.11
  94.8 10.0 %all-to-all-done.1 = f32[8,128,128]{2,1,0:T(8,128)S(1)} async-done(((f32[8,128,128]{2,1,0:T(8,128)}), f32[8,128,128]{2,1,0:T(8,128)S(1)}, u32[]{:S(2)}, u32[]{:S(2)}) %all-to-all-start.1) | async-done | bytes 524320 | tf_op jit(solution)/shard_map/all_to_all | solution.py:59
  104.8 0.2 multiply_reduce_fusion
  105.0 0.7 divide_convert_fusion
  (20 shorter events, 0.4 us)
Async XLA Ops:
  6.5 50.8 %all-reduce.3.cloned.1.call-start = ((), (), s32[]{:S(2)}) async-start(), calls=%async_computation.3 | async-start | bytes 4194304 | tf_op jit(solution)/shard_map/psum | solution.py:11
  72.5 9.6 %all-to-all-start = ((f32[8,128,1]{1,2,0:T(1,128)}), f32[8,128,1]{1,2,0:T(1,128)S(1)}, u32[]{:S(2)}, u32[]{:S(2)}) async-start(f32[8,128,1]{1,2,0:T(1,128)} %all_to_all.18), calls=%async_computation | async-start | bytes 8192 | tf_op jit(solution)/shard_map/all_to_all | solution.py:57
  91.1 13.7 %all-to-all-start.1 = ((f32[8,128,128]{2,1,0:T(8,128)}), f32[8,128,128]{2,1,0:T(8,128)S(1)}, u32[]{:S(2)}, u32[]{:S(2)}) async-start(f32[8,128,128]{2,1,0:T(8,128)} %bitcast.13), calls=%async_computation.1 | async-start | bytes 1048576 | tf_op jit(solution)/shard_map/all_to_all | solution.py:59
Sparse Core Ops, SparseCore 0:
  10.4 23.4 all-reduce.2
where the time goes:
time: 112 us; the launch traced here: 113 us
  blocking collectives  53.1 us (47%)
  waiting for transfers between devices  16.4 us (15%)
  between operations  14.7 us (13%)
  other arithmetic  9.46 us (8%)
  matrix products  7.22 us (6%)
  starting transfers between devices  6.8 us (6%)
  local copies, waits for them, and re-layouts  4.86 us (4%)
    all_gather x1, blocking collectives, per_device(): every_query = lax.all_gather(query_rows, 'ctx', axis=0, tiled=True)  31.1 us
    unnamed x1, blocking collectives  13.1 us
    all_to_all x1, waiting for transfers between devices, per_device(): lax.all_to_all(partials, 'ctx', split_axis=0, concat_axis=0, tiled=True)  10 us
    all_to_all x1, blocking collectives, per_device(): lax.all_to_all(totals, 'ctx', split_axis=0, concat_axis=0, tiled=True)  9 us
    all_to_all x1, waiting for transfers between devices, per_device(): lax.all_to_all(tops, 'ctx', split_axis=0, concat_axis=0, tiled=True)  6.31 us
    reduce_sum x2, other arithmetic, shard_partials(): total = jnp.sum(weights.astype(jnp.float32), axis=1)  5.43 us
    dot_general x2, matrix products, shard_partials(): partial_value = jnp.dot(weights, values, preferred_element_type=jnp.float32)  3.9 us
    all_to_all x1, starting transfers between devices, per_device(): lax.all_to_all(partials, 'ctx', split_axis=0, concat_axis=0, tiled=True)  3.49 us
  transfers between devices with their start and end apart: 3, of which 2 were waited for; matrix products, arithmetic and copies ran while one was open for 2% of the time, Pallas kernels for 0%

commit v1 on v0

v1 whole, which is shorter than its diff:
```python
import functools
import math

import jax
import jax.numpy as jnp
from jax import lax
from jax.experimental import pallas as pl
from jax.experimental.pallas import tpu as pltpu
from jax.sharding import PartitionSpec as P

MESH = pl.DeviceIdType.MESH
KEYS = 256
DEPTH = 1024


def distance(slot, count):
    return count // 2 + (1 - 2 * (slot % 2)) * ((slot + 1) // 2)


def kernel(
    count, heads, pack,
    q_ref, cache_ref, owner_ref, len_ref, out_ref,
    own_kv, got_kv, k_buf, v_buf, q_buf, len_buf, len_out, s_buf, snd, rcv,
    kv_send, kv_recv, kv_local, q_send, q_recv, l_send, l_recv, o_send, o_recv,
):
    me = lax.axis_index("ctx")
    rep = lax.axis_index("rep")
    rows, width = q_ref.shape
    reqs = rows // heads
    span = cache_ref.shape[2]
    factor = width ** (-0.5) * math.log2(math.e)
    other = 1 - rep

    locals_ = [
        pltpu.make_async_copy(cache_ref.at[0, i], own_kv.at[i], kv_local.at[i]) for i in range(2)
    ]
    for copy in locals_:
        copy.start()

    barrier = pltpu.get_barrier_semaphore()
    for t in range(1, count):
        pl.semaphore_signal(
            barrier, inc=1, device_id={"ctx": (me + t) % count}, device_id_type=MESH
        )
    pl.semaphore_signal(barrier, inc=1, device_id={"rep": other}, device_id_type=MESH)

    for i in range(reqs):
        len_out[i : i + 1, :] = jnp.full((1, 128), len_ref[i], jnp.int32)
    len_buf[count - 1] = len_out[...]
    q_buf[count - 1] = q_ref[...]
    v_buf[:, width:] = jnp.ones((span, width), jnp.bfloat16)
    pl.semaphore_wait(barrier, count)

    kv = [
        pltpu.make_async_remote_copy(
            src_ref=cache_ref.at[0, i], dst_ref=got_kv.at[i],
            send_sem=kv_send.at[i], recv_sem=kv_recv.at[i],
            device_id={"rep": other}, device_id_type=MESH,
        )
        for i in range(2)
    ]
    qs, ls = [], []
    for j in range(count - 1):
        peer = {"ctx": (me + count - distance(j, count)) % count}
        qs.append(pltpu.make_async_remote_copy(
            src_ref=q_ref, dst_ref=q_buf.at[j], send_sem=q_send.at[j], recv_sem=q_recv.at[j],
            device_id=peer, device_id_type=MESH,
        ))
        ls.append(pltpu.make_async_remote_copy(
            src_ref=len_out, dst_ref=len_buf.at[j], send_sem=l_send.at[j], recv_sem=l_recv.at[j],
            device_id=peer, device_id_type=MESH,
        ))
    for copy in kv:
        copy.start()
    for a, b in zip(qs, ls):
        a.start()
        b.start()

    diff = owner_ref[0] - rep
    keep = 1 - diff * diff
    mine = jnp.full((1, width), keep, jnp.int32).astype(jnp.float32).astype(jnp.bfloat16)
    theirs = jnp.full((1, width), 1 - keep, jnp.int32).astype(jnp.float32).astype(jnp.bfloat16)
    locals_[0].wait()
    kv[0].wait_recv()
    k_buf[...] = own_kv[0] * mine + got_kv[0] * theirs
    locals_[1].wait()
    kv[1].wait_recv()
    v_buf[:, :width] = own_kv[1] * mine + got_kv[1] * theirs
    for a, b in zip(qs, ls):
        a.wait_recv()
        b.wait_recv()

    def partial_copy(j):
        return pltpu.make_async_remote_copy(
            src_ref=snd.at[j], dst_ref=rcv.at[j], send_sem=o_send.at[j], recv_sem=o_recv.at[j],
            device_id={"ctx": (me + distance(j, count)) % count}, device_id_type=MESH,
        )

    big = pack * rows
    start = me * span
    lane = lax.broadcasted_iota(jnp.int32, (big, 128), 1)
    first_lane = lax.broadcasted_iota(jnp.int32, (rows, 128), 1) == 0

    def step(g, carry):
        q = q_buf[pl.ds(g * pack, pack)].reshape(big, width)
        lens = len_buf[pl.ds(g * pack, pack)]
        left = jnp.broadcast_to(
            lens.reshape(pack * reqs, 1, 128), (pack * reqs, heads, 128)
        ).reshape(big, 128) - start - lane
        top = jnp.full((big, 128), -1e30, jnp.float32)
        for k in range(span // KEYS):
            s = lax.dot_general(
                q, k_buf[k * KEYS : (k + 1) * KEYS, :], (((1,), (1,)), ((), ())),
                preferred_element_type=jnp.float32,
            )
            for i in range(KEYS // 128):
                at = k * KEYS + i * 128
                part = jnp.where(left > at, s[:, i * 128 : (i + 1) * 128], jnp.float32(-1e30))
                s_buf[:, at : at + 128] = part
                top = jnp.maximum(top, part)
        top = jnp.max(top, axis=1, keepdims=True)
        acc = None
        for k in range(span // DEPTH):
            at = k * DEPTH
            w = jnp.exp2((s_buf[:, at : at + DEPTH] - top) * factor).astype(jnp.bfloat16)
            term = jnp.dot(w, v_buf[at : at + DEPTH, :], preferred_element_type=jnp.float32)
            acc = term if acc is None else acc + term
        for i in range(pack):
            j = g * pack + i
            here = acc[i * rows : (i + 1) * rows]
            stats = jnp.where(first_lane, top[i * rows : (i + 1) * rows], here[:, width:])
            snd[j, :rows, :] = here[:, :width]
            snd[j, rows:, :] = jnp.transpose(stats)[:8]

            @pl.when(j < count - 1)
            def _():
                partial_copy(j).start()

        return carry

    lax.fori_loop(0, count // pack, step, 0)

    for copy in kv:
        copy.wait_send()
    for a, b in zip(qs, ls):
        a.wait_send()
        b.wait_send()
    copies = [partial_copy(j) for j in range(count - 1)]
    for copy in copies:
        copy.wait_recv()
    slots = [rcv.at[j] for j in range(count - 1)] + [snd.at[count - 1]]
    tops, totals = [], []
    for slot in slots:
        turned = jnp.transpose(slot[rows:, :])
        tops.append(turned[:, 0:1])
        totals.append(turned[:, 1:2])
    top = functools.reduce(jnp.maximum, tops)
    total = jnp.zeros((rows, 1), jnp.float32)
    value = jnp.zeros((rows, width), jnp.float32)
    for slot, t, l in zip(slots, tops, totals):
        e = jnp.exp2((t - top) * factor)
        total = total + e * l
        value = value + e * slot[:rows, :]
    out_ref[...] = (value / total).astype(jnp.bfloat16)
    for copy in copies:
        copy.wait_send()


def per_device(queries, cache, owner, lengths):
    count = lax.axis_size("ctx")
    req, heads, width = queries.shape
    rows = req * heads
    span = cache.shape[2]
    pack = 2
    big = pack * rows
    vmem = pl.BlockSpec(memory_space=pltpu.VMEM)
    smem = pl.BlockSpec(memory_space=pltpu.SMEM)
    dma = pltpu.SemaphoreType.DMA
    out = pl.pallas_call(
        functools.partial(kernel, count, heads, pack),
        out_shape=jax.ShapeDtypeStruct((rows, width), jnp.bfloat16),
        in_specs=[vmem, pl.BlockSpec(memory_space=pl.ANY), smem, smem],
        out_specs=vmem,
        scratch_shapes=[
            pltpu.VMEM((2, span, width), jnp.bfloat16),
            pltpu.VMEM((2, span, width), jnp.bfloat16),
            pltpu.VMEM((span, width), jnp.bfloat16),
            pltpu.VMEM((span, 2 * width), jnp.bfloat16),
            pltpu.VMEM((count, rows, width), jnp.bfloat16),
            pltpu.VMEM((count, req, 128), jnp.int32),
            pltpu.VMEM((req, 128), jnp.int32),
            pltpu.VMEM((big, span), jnp.float32),
            pltpu.VMEM((count, rows + 8, width), jnp.float32),
            pltpu.VMEM((count, rows + 8, width), jnp.float32),
            dma((2,)), dma((2,)), dma((2,)),
            dma((count - 1,)), dma((count - 1,)),
            dma((count - 1,)), dma((count - 1,)),
            dma((count - 1,)), dma((count - 1,)),
        ],
        compiler_params=pltpu.CompilerParams(
            collective_id=0, has_side_effects=True, vmem_limit_bytes=48 * 1024 * 1024
        ),
    )(queries.reshape(rows, width), cache, owner, lengths)
    return out.reshape(req, heads, width)


def solution(mesh):
    placed = (
        P(("groups", "ctx", "rep"), None, None),
        P("rep", None, ("groups", "ctx"), None),
        P(("groups", "ctx")),
        P(("groups", "ctx", "rep")),
    )
    return jax.shard_map(
        per_device,
        mesh=mesh,
        in_specs=placed,
        out_specs=P(("groups", "ctx", "rep"), None, None),
        check_vma=False,
    )
```

time: 112 us -> 34.1 us (0.30)
  blocking collectives: 53.1 us -> 0 us
  Pallas kernels: 0 us -> 29.6 us
  waiting for transfers between devices: 16.4 us -> 0 us
  between operations: 14.7 us -> 0.67 us
  other arithmetic: 9.46 us -> 0 us
  matrix products: 7.22 us -> 0 us
  starting transfers between devices: 6.8 us -> 0 us
  local copies, waits for them, and re-layouts: 4.86 us -> 3.61 us
    all_gather x1 -> x0, blocking collectives: 31.1 us -> none  [per_device(): every_query = lax.all_gather(query_rows, 'ctx', axis=0, tiled=True)]
    pallas_call x0 -> x1, Pallas kernels: none -> 29.6 us  [per_device(): pl.pallas_call(functools.partial(kernel, count, heads, pack), out_shape=j...]
    all_to_all x2 -> x0, waiting for transfers between devices: 16.4 us -> none  [the longest x1 10 us: per_device(): lax.all_to_all(partials, 'ctx', split_axis=0, concat_axis=0, tiled=True)]
    unnamed x1 -> x0, blocking collectives: 13.1 us -> none
    all_to_all x1 -> x0, blocking collectives: 9 us -> none  [per_device(): lax.all_to_all(totals, 'ctx', split_axis=0, concat_axis=0, tiled=True)]
    dot_general x4 -> x0, matrix products: 7.22 us -> none  [the longest x2 3.9 us: shard_partials(): partial_value = jnp.dot(weights, values, preferred_element_type=jnp.float32)]
    all_to_all x2 -> x0, starting transfers between devices: 6.8 us -> none  [the longest x1 3.49 us: per_device(): lax.all_to_all(partials, 'ctx', split_axis=0, concat_axis=0, tiled=True)]
    reduce_sum x4 -> x0, other arithmetic: 5.65 us -> none  [the longest x2 5.43 us: shard_partials(): total = jnp.sum(weights.astype(jnp.float32), axis=1)]
  transfers between devices with their start and end apart: 3 -> 0, of which waited for: 2 -> 0; matrix products, arithmetic and copies ran while one was open for 2% -> 0% of each run, Pallas kernels for 0% -> 0%
where the time goes in v1:
time: 34.1 us; the launch traced here: 33.9 us
  Pallas kernels  29.6 us (87%)
  local copies, waits for them, and re-layouts  3.61 us (11%)
  between operations  0.67 us (2%)
    pallas_call x1, Pallas kernels, per_device(): pl.pallas_call(functools.partial(kernel, count, heads, pack), out_shape=j...  29.6 us
    unnamed x7, local copies, waits for them, and re-layouts  3.61 us

profile of v1, /device:TPU:0, one launch (start us, length us, event | category | flops | bytes accessed | tf_op | source)
XLA Modules:
  0.0 33.9 jit_solution(13877615833837875624)
XLA Ops:
  0.7 0.0 copy-start
  0.7 1.6 %copy-done = bf16[1,2,4096,128]{3,2,1,0:T(8,128)(2,1)S(1)} copy-done((bf16[1,2,4096,128]{3,2,1,0:T(8,128)(2,1)S(1)}, bf16[1,2,4096,128]{3,2,1,0:T(8,128)(2,1)}, u32[]{:S(2)}) %copy-start) | copy-done | bytes 2097176
  2.2 0.0 copy-start.1
  2.2 0.8 %copy-done.1 = bf16[8,16,128]{2,1,0:T(8,128)(2,1)S(1)} copy-done((bf16[8,16,128]{2,1,0:T(8,128)(2,1)S(1)}, bf16[8,16,128]{2,1,0:T(8,128)(2,1)}, u32[]{:S(2)}) %copy-start.1) | copy-done | bytes 32792
  3.0 0.0 copy-start.2
  3.0 0.7 %copy-done.2 = s32[8]{0:T(128)S(1)} copy-done((s32[8]{0:T(128)S(1)}, s32[8]{0:T(128)}, u32[]{:S(2)}) %copy-start.2) | copy-done | bytes 56
  3.7 29.6 %shard_map.46 = bf16[128,128]{1,0:T(8,128)(2,1)S(1)} custom-call(bf16[128,128]{1,0:T(8,128)(2,1)S(1)} %bitcast.3, bf16[1,2,4096,128]{3,2,1,0:T(8,128)(2,1)S(1)} %copy-done, s32[1]{0:T(128)S(6)} %copy.6.owner_ref, s32[8]{0:T(128)S(1)} %copy-done.2), custom_call_target="tpu_custom_call" | custom-call | tf_op jit(solution)/shard_map/pallas_call | solution.py:179
  33.3 0.6 %copy.7 = bf16[8,16,128]{2,1,0:T(8,128)(2,1)} copy(bf16[8,16,128]{2,1,0:T(8,128)(2,1)S(1)} %bitcast.2) | data formatting | bytes 65536
Async XLA Ops:
  0.7 1.6 %copy-start = (bf16[1,2,4096,128]{3,2,1,0:T(8,128)(2,1)S(1)}, bf16[1,2,4096,128]{3,2,1,0:T(8,128)(2,1)}, u32[]{:S(2)}) copy-start(bf16[1,2,4096,128]{3,2,1,0:T(8,128)(2,1)} %cache_ref.1) | copy-start | bytes 6291460
  2.2 0.8 %copy-start.1 = (bf16[8,16,128]{2,1,0:T(8,128)(2,1)S(1)}, bf16[8,16,128]{2,1,0:T(8,128)(2,1)}, u32[]{:S(2)}) copy-start(bf16[8,16,128]{2,1,0:T(8,128)(2,1)} %param.4) | copy-start | bytes 98308
  3.0 0.7 %copy-start.2 = (s32[8]{0:T(128)S(1)}, s32[8]{0:T(128)}, u32[]{:S(2)}) copy-start(s32[8]{0:T(128)} %len_ref.1) | copy-start | bytes 100

commit v2 on v1

--- a/solution.py
+++ b/solution.py
@@ -19,9 +19,9 @@
 
 def kernel(
     count, heads, pack,
-    q_ref, cache_ref, owner_ref, len_ref, out_ref,
-    own_kv, got_kv, k_buf, v_buf, q_buf, len_buf, len_out, s_buf, snd, rcv,
-    kv_send, kv_recv, kv_local, q_send, q_recv, l_send, l_recv, o_send, o_recv,
+    q_ref, cache_ref, owner_hbm, len_hbm, out_ref,
+    own_kv, got_kv, k_buf, v_buf, q_buf, len_buf, len_out, s_buf, snd, mid, rcv,
+    owner_ref, len_ref, kv_send, kv_recv, kv_local, q_send, q_recv, l_send, l_recv, o_send, o_recv,
 ):
     me = lax.axis_index("ctx")
     rep = lax.axis_index("rep")
@@ -30,11 +30,22 @@
     span = cache_ref.shape[2]
     factor = width ** (-0.5) * math.log2(math.e)
     other = 1 - rep
+    half = count // 2
+    outer, inner = me // 2, me % 2
+    beside = outer * 2 + 1 - inner
+
+    def shifted(d, parity):
+        return ((outer + half + d) % half) * 2 + parity
 
     locals_ = [
         pltpu.make_async_copy(cache_ref.at[0, i], own_kv.at[i], kv_local.at[i]) for i in range(2)
     ]
-    for copy in locals_:
+    small = [
+        pltpu.make_async_copy(len_hbm, len_ref, kv_local.at[2]),
+        pltpu.make_async_copy(owner_hbm, owner_ref, kv_local.at[3]),
+        pltpu.make_async_copy(q_ref, q_buf.at[count - 1], kv_local.at[4]),
+    ]
+    for copy in small + locals_:
         copy.start()
 
     barrier = pltpu.get_barrier_semaphore()
@@ -44,10 +55,11 @@
         )
     pl.semaphore_signal(barrier, inc=1, device_id={"rep": other}, device_id_type=MESH)
 
+    for copy in small:
+        copy.wait()
     for i in range(reqs):
         len_out[i : i + 1, :] = jnp.full((1, 128), len_ref[i], jnp.int32)
     len_buf[count - 1] = len_out[...]
-    q_buf[count - 1] = q_ref[...]
     v_buf[:, width:] = jnp.ones((span, width), jnp.bfloat16)
     pl.semaphore_wait(barrier, count)
 
@@ -59,22 +71,33 @@
         )
         for i in range(2)
     ]
-    qs, ls = [], []
+    qs, forwards, ls = [], [], []
     for j in range(count - 1):
-        peer = {"ctx": (me + count - distance(j, count)) % count}
-        qs.append(pltpu.make_async_remote_copy(
-            src_ref=q_ref, dst_ref=q_buf.at[j], send_sem=q_send.at[j], recv_sem=q_recv.at[j],
-            device_id=peer, device_id_type=MESH,
-        ))
+        d = distance(j % half, half)
+        parity = 1 - inner if j < half else inner
         ls.append(pltpu.make_async_remote_copy(
             src_ref=len_out, dst_ref=len_buf.at[j], send_sem=l_send.at[j], recv_sem=l_recv.at[j],
-            device_id=peer, device_id_type=MESH,
+            device_id={"ctx": shifted(-d, parity)}, device_id_type=MESH,
+        ))
+        if j >= half:
+            qs.append(pltpu.make_async_remote_copy(
+                src_ref=q_ref, dst_ref=q_buf.at[j],
+                send_sem=q_send.at[j], recv_sem=q_recv.at[j],
+                device_id={"ctx": shifted(-d, inner)}, device_id_type=MESH,
+            ))
+    for i in range(half):
+        forwards.append(pltpu.make_async_remote_copy(
+            src_ref=q_buf.at[half + i], dst_ref=q_buf.at[i],
+            send_sem=q_send.at[i], recv_sem=q_recv.at[i],
+            device_id={"ctx": beside}, device_id_type=MESH,
         ))
     for copy in kv:
         copy.start()
-    for a, b in zip(qs, ls):
-        a.start()
-        b.start()
+    for copy in qs + ls + forwards[half - 1 :]:
+        copy.start()
+    for i in list(range(1, half - 1)) + [0]:
+        qs[i].wait_recv()
+        forwards[i].start()
 
     diff = owner_ref[0] - rep
     keep = 1 - diff * diff
@@ -86,14 +109,20 @@
     locals_[1].wait()
     kv[1].wait_recv()
     v_buf[:, :width] = own_kv[1] * mine + got_kv[1] * theirs
-    for a, b in zip(qs, ls):
-        a.wait_recv()
-        b.wait_recv()
-
-    def partial_copy(j):
+    for copy in forwards + ls:
+        copy.wait_recv()
+
+    def pair_copy(i):
         return pltpu.make_async_remote_copy(
-            src_ref=snd.at[j], dst_ref=rcv.at[j], send_sem=o_send.at[j], recv_sem=o_recv.at[j],
-            device_id={"ctx": (me + distance(j, count)) % count}, device_id_type=MESH,
+            src_ref=snd.at[i], dst_ref=mid.at[i], send_sem=o_send.at[i], recv_sem=o_recv.at[i],
+            device_id={"ctx": beside}, device_id_type=MESH,
+        )
+
+    def final_copy(i):
+        j = half + i
+        return pltpu.make_async_remote_copy(
+            src_ref=snd.at[j], dst_ref=rcv.at[i], send_sem=o_send.at[j], recv_sem=o_recv.at[j],
+            device_id={"ctx": shifted(distance(i, half), inner)}, device_id_type=MESH,
         )
 
     big = pack * rows
@@ -101,7 +130,7 @@
     lane = lax.broadcasted_iota(jnp.int32, (big, 128), 1)
     first_lane = lax.broadcasted_iota(jnp.int32, (rows, 128), 1) == 0
 
-    def step(g, carry):
+    def partials(g):
         q = q_buf[pl.ds(g * pack, pack)].reshape(big, width)
         lens = len_buf[pl.ds(g * pack, pack)]
         left = jnp.broadcast_to(
@@ -125,30 +154,51 @@
             w = jnp.exp2((s_buf[:, at : at + DEPTH] - top) * factor).astype(jnp.bfloat16)
             term = jnp.dot(w, v_buf[at : at + DEPTH, :], preferred_element_type=jnp.float32)
             acc = term if acc is None else acc + term
-        for i in range(pack):
+        return [(top[i * rows : (i + 1) * rows], acc[i * rows : (i + 1) * rows]) for i in range(pack)]
+
+    def put(j, top, total, value):
+        snd[j, :rows, :] = value
+        snd[j, rows:, :] = jnp.transpose(jnp.where(first_lane, top, total))[:8]
+
+    def first(g, carry):
+        for i, (top, acc) in enumerate(partials(g)):
             j = g * pack + i
-            here = acc[i * rows : (i + 1) * rows]
-            stats = jnp.where(first_lane, top[i * rows : (i + 1) * rows], here[:, width:])
-            snd[j, :rows, :] = here[:, :width]
-            snd[j, rows:, :] = jnp.transpose(stats)[:8]
-
-            @pl.when(j < count - 1)
+            put(j, top, acc[:, width:], acc[:, :width])
+            pair_copy(j).start()
+        return carry
+
+    def second(g, carry):
+        for i, (top, acc) in enumerate(partials(half // pack + g)):
+            j = g * pack + i
+            pair_copy(j).wait_recv()
+            turned = jnp.transpose(mid[j, rows:, :])
+            best = jnp.maximum(top, turned[:, 0:1])
+            here = jnp.exp2((top - best) * factor)
+            there = jnp.exp2((turned[:, 0:1] - best) * factor)
+            put(
+                half + j,
+                best,
+                acc[:, width:] * here + turned[:, 1:2] * there,
+                acc[:, :width] * here + mid[j, :rows, :] * there,
+            )
+
+            @pl.when(j < half - 1)
             def _():
-                partial_copy(j).start()
+                final_copy(j).start()
 
         return carry
 
-    lax.fori_loop(0, count // pack, step, 0)
-
-    for copy in kv:
+    lax.fori_loop(0, half // pack, first, 0)
+    lax.fori_loop(0, half // pack, second, 0)
+
+    for copy in kv + qs + ls + forwards:
         copy.wait_send()
-    for a, b in zip(qs, ls):
-        a.wait_send()
-        b.wait_send()
-    copies = [partial_copy(j) for j in range(count - 1)]
+    for i in range(half):
+        pair_copy(i).wait_send()
+    copies = [final_copy(i) for i in range(half - 1)]
     for copy in copies:
         copy.wait_recv()
-    slots = [rcv.at[j] for j in range(count - 1)] + [snd.at[count - 1]]
+    slots = [rcv.at[i] for i in range(half - 1)] + [snd.at[count - 1]]
     tops, totals = [], []
     for slot in slots:
         turned = jnp.transpose(slot[rows:, :])
@@ -174,12 +224,12 @@
     pack = 2
     big = pack * rows
     vmem = pl.BlockSpec(memory_space=pltpu.VMEM)
-    smem = pl.BlockSpec(memory_space=pltpu.SMEM)
+    hbm = pl.BlockSpec(memory_space=pltpu.HBM)
     dma = pltpu.SemaphoreType.DMA
     out = pl.pallas_call(
         functools.partial(kernel, count, heads, pack),
         out_shape=jax.ShapeDtypeStruct((rows, width), jnp.bfloat16),
-        in_specs=[vmem, pl.BlockSpec(memory_space=pl.ANY), smem, smem],
+        in_specs=[hbm] * 4,
         out_specs=vmem,
         scratch_shapes=[
             pltpu.VMEM((2, span, width), jnp.bfloat16),
@@ -191,14 +241,17 @@
             pltpu.VMEM((req, 128), jnp.int32),
             pltpu.VMEM((big, span), jnp.float32),
             pltpu.VMEM((count, rows + 8, width), jnp.float32),
-            pltpu.VMEM((count, rows + 8, width), jnp.float32),
-            dma((2,)), dma((2,)), dma((2,)),
+            pltpu.VMEM((count // 2, rows + 8, width), jnp.float32),
+            pltpu.VMEM((count // 2, rows + 8, width), jnp.float32),
+            pltpu.SMEM((1,), jnp.int32),
+            pltpu.SMEM((req,), jnp.int32),
+            dma((2,)), dma((2,)), dma((5,)),
             dma((count - 1,)), dma((count - 1,)),
             dma((count - 1,)), dma((count - 1,)),
             dma((count - 1,)), dma((count - 1,)),
         ],
         compiler_params=pltpu.CompilerParams(
-            collective_id=0, has_side_effects=True, vmem_limit_bytes=48 * 1024 * 1024
+            collective_id=0, has_side_effects=True, vmem_limit_bytes=63 * 1024 * 1024
         ),
     )(queries.reshape(rows, width), cache, owner, lengths)
     return out.reshape(req, heads, width)

time: 34.1 us -> 31.7 us (0.930)
  local copies, waits for them, and re-layouts: 3.61 us -> 1.38 us
    unnamed x7 -> x1, local copies, waits for them, and re-layouts: 3.61 us -> 1.38 us
where the time goes in v2:
time: 31.7 us; the launch traced here: 31.5 us
  Pallas kernels  29.5 us (93%)
  local copies, waits for them, and re-layouts  1.38 us (4%)
  between operations  0.66 us (2%)
    pallas_call x1, Pallas kernels, per_device(): pl.pallas_call(functools.partial(kernel, count, heads, pack), out_shape=j...  29.5 us
    unnamed x1, local copies, waits for them, and re-layouts  1.38 us

profile of v2, /device:TPU:0, one launch (start us, length us, event | category | flops | bytes accessed | tf_op | source)
XLA Modules:
  0.0 31.5 jit_solution(2302254345134391600)
XLA Ops:
  0.7 29.5 %shard_map.46 = bf16[128,128]{1,0:T(8,128)(2,1)} custom-call(bf16[128,128]{1,0:T(8,128)(2,1)} %bitcast.3, bf16[1,2,4096,128]{3,2,1,0:T(8,128)(2,1)} %cache_ref.1, s32[1]{0:T(128)S(6)} %copy.6.owner_hbm, s32[8]{0:T(128)} %len_hbm.1), custom_call_target="tpu_custom_call" | custom-call | tf_op jit(solution)/shard_map/pallas_call | solution.py:229
  30.2 1.4 %copy.7 = bf16[8,16,128]{2,1,0:T(8,128)(2,1)} copy(bf16[8,16,128]{2,1,0:T(8,128)(2,1)} %bitcast.2) | data formatting | bytes 65536

commit v3 on v2

--- a/solution.py
+++ b/solution.py
@@ -20,7 +20,7 @@
 def kernel(
     count, heads, pack,
     q_ref, cache_ref, owner_hbm, len_hbm, out_ref,
-    own_kv, got_kv, k_buf, v_buf, q_buf, len_buf, len_out, s_buf, snd, mid, rcv,
+    own_kv, got_kv, k_buf, v_buf, q_buf, len_buf, len_out, s_buf, top_buf, snd, mid, rcv,
     owner_ref, len_ref, kv_send, kv_recv, kv_local, q_send, q_recv, l_send, l_recv, o_send, o_recv,
 ):
     me = lax.axis_index("ctx")
@@ -72,28 +72,27 @@
         for i in range(2)
     ]
     qs, forwards, ls = [], [], []
-    for j in range(count - 1):
-        d = distance(j % half, half)
-        parity = 1 - inner if j < half else inner
-        ls.append(pltpu.make_async_remote_copy(
-            src_ref=len_out, dst_ref=len_buf.at[j], send_sem=l_send.at[j], recv_sem=l_recv.at[j],
-            device_id={"ctx": shifted(-d, parity)}, device_id_type=MESH,
-        ))
-        if j >= half:
+    for i in range(half):
+        d = distance(i, half)
+        targets = [(2 * i, 1 - inner), (2 * i + 1, inner)]
+        for j, parity in targets if i < half - 1 else targets[:1]:
+            ls.append(pltpu.make_async_remote_copy(
+                src_ref=len_out, dst_ref=len_buf.at[j],
+                send_sem=l_send.at[j], recv_sem=l_recv.at[j],
+                device_id={"ctx": shifted(-d, parity)}, device_id_type=MESH,
+            ))
+        if i < half - 1:
             qs.append(pltpu.make_async_remote_copy(
-                src_ref=q_ref, dst_ref=q_buf.at[j],
-                send_sem=q_send.at[j], recv_sem=q_recv.at[j],
+                src_ref=q_ref, dst_ref=q_buf.at[2 * i + 1],
+                send_sem=q_send.at[2 * i + 1], recv_sem=q_recv.at[2 * i + 1],
                 device_id={"ctx": shifted(-d, inner)}, device_id_type=MESH,
             ))
-    for i in range(half):
         forwards.append(pltpu.make_async_remote_copy(
-            src_ref=q_buf.at[half + i], dst_ref=q_buf.at[i],
-            send_sem=q_send.at[i], recv_sem=q_recv.at[i],
+            src_ref=q_buf.at[2 * i + 1], dst_ref=q_buf.at[2 * i],
+            send_sem=q_send.at[2 * i], recv_sem=q_recv.at[2 * i],
             device_id={"ctx": beside}, device_id_type=MESH,
         ))
-    for copy in kv:
-        copy.start()
-    for copy in qs + ls + forwards[half - 1 :]:
+    for copy in qs + ls + forwards[half - 1 :] + kv:
         copy.start()
     for i in list(range(1, half - 1)) + [0]:
         qs[i].wait_recv()
@@ -106,20 +105,18 @@
     locals_[0].wait()
     kv[0].wait_recv()
     k_buf[...] = own_kv[0] * mine + got_kv[0] * theirs
-    locals_[1].wait()
-    kv[1].wait_recv()
-    v_buf[:, :width] = own_kv[1] * mine + got_kv[1] * theirs
     for copy in forwards + ls:
         copy.wait_recv()
 
     def pair_copy(i):
         return pltpu.make_async_remote_copy(
-            src_ref=snd.at[i], dst_ref=mid.at[i], send_sem=o_send.at[i], recv_sem=o_recv.at[i],
+            src_ref=snd.at[2 * i], dst_ref=mid.at[i],
+            send_sem=o_send.at[2 * i], recv_sem=o_recv.at[2 * i],
             device_id={"ctx": beside}, device_id_type=MESH,
         )
 
     def final_copy(i):
-        j = half + i
+        j = 2 * i + 1
         return pltpu.make_async_remote_copy(
             src_ref=snd.at[j], dst_ref=rcv.at[i], send_sem=o_send.at[j], recv_sem=o_recv.at[j],
             device_id={"ctx": shifted(distance(i, half), inner)}, device_id_type=MESH,
@@ -130,66 +127,95 @@
     lane = lax.broadcasted_iota(jnp.int32, (big, 128), 1)
     first_lane = lax.broadcasted_iota(jnp.int32, (rows, 128), 1) == 0
 
-    def partials(g):
+    def scoring(g):
         q = q_buf[pl.ds(g * pack, pack)].reshape(big, width)
         lens = len_buf[pl.ds(g * pack, pack)]
         left = jnp.broadcast_to(
             lens.reshape(pack * reqs, 1, 128), (pack * reqs, heads, 128)
         ).reshape(big, 128) - start - lane
-        top = jnp.full((big, 128), -1e30, jnp.float32)
-        for k in range(span // KEYS):
+        return q, left
+
+    def score(q, left, top, begin, end):
+        for k in range(begin, end, KEYS):
             s = lax.dot_general(
-                q, k_buf[k * KEYS : (k + 1) * KEYS, :], (((1,), (1,)), ((), ())),
+                q, k_buf[k : k + KEYS, :], (((1,), (1,)), ((), ())),
                 preferred_element_type=jnp.float32,
             )
-            for i in range(KEYS // 128):
-                at = k * KEYS + i * 128
-                part = jnp.where(left > at, s[:, i * 128 : (i + 1) * 128], jnp.float32(-1e30))
+            for at in range(k, k + KEYS, 128):
+                part = jnp.where(left > at, s[:, at - k : at - k + 128], jnp.float32(-1e30))
                 s_buf[:, at : at + 128] = part
                 top = jnp.maximum(top, part)
-        top = jnp.max(top, axis=1, keepdims=True)
-        acc = None
-        for k in range(span // DEPTH):
-            at = k * DEPTH
-            w = jnp.exp2((s_buf[:, at : at + DEPTH] - top) * factor).astype(jnp.bfloat16)
-            term = jnp.dot(w, v_buf[at : at + DEPTH, :], preferred_element_type=jnp.float32)
-            acc = term if acc is None else acc + term
-        return [(top[i * rows : (i + 1) * rows], acc[i * rows : (i + 1) * rows]) for i in range(pack)]
+        return top
+
+    def weigh(top, acc, at):
+        w = jnp.concatenate(
+            [
+                jnp.exp2((s_buf[:, i : i + 128] - top) * factor).astype(jnp.bfloat16)
+                for i in range(at, at + DEPTH, 128)
+            ],
+            axis=1,
+        )
+        term = jnp.dot(w, v_buf[at : at + DEPTH, :], preferred_element_type=jnp.float32)
+        return term if acc is None else acc + term
+
+    def spread(top):
+        return jnp.broadcast_to(jnp.max(top, axis=1, keepdims=True), (big, 128))
 
     def put(j, top, total, value):
         snd[j, :rows, :] = value
         snd[j, rows:, :] = jnp.transpose(jnp.where(first_lane, top, total))[:8]
 
-    def first(g, carry):
-        for i, (top, acc) in enumerate(partials(g)):
-            j = g * pack + i
-            put(j, top, acc[:, width:], acc[:, :width])
-            pair_copy(j).start()
+    def ship(g, top, acc):
+        for i in range(pack):
+            at = slice(i * rows, (i + 1) * rows)
+            put(g * pack + i, top[at], acc[at, width:], acc[at, :width])
+            if i == 0:
+                pair_copy(g).start()
+
+    def merge(g):
+        j = 2 * g + 1
+        pair_copy(g).wait_recv()
+        mine_ = jnp.transpose(snd[j, rows:, :])
+        theirs_ = jnp.transpose(mid[g, rows:, :])
+        best = jnp.maximum(mine_[:, 0:1], theirs_[:, 0:1])
+        here = jnp.exp2((mine_[:, 0:1] - best) * factor)
+        there = jnp.exp2((theirs_[:, 0:1] - best) * factor)
+        put(
+            j, best, mine_[:, 1:2] * here + theirs_[:, 1:2] * there,
+            snd[j, :rows, :] * here + mid[g, :rows, :] * there,
+        )
+
+    floor = jnp.full((big, 128), -1e30, jnp.float32)
+    top_buf[...] = spread(score(*scoring(0), floor, 0, span))
+    locals_[1].wait()
+    kv[1].wait_recv()
+    v_buf[:, :width] = own_kv[1] * mine + got_kv[1] * theirs
+
+    def step(g, carry):
+        top, acc, later = top_buf[...], None, floor
+        q, left = scoring(g + 1)
+        for at in range(0, span, DEPTH):
+            acc = weigh(top, acc, at)
+            later = score(q, left, later, at, at + DEPTH)
+        top_buf[...] = spread(later)
+        ship(g, top, acc)
+
+        @pl.when(g > 0)
+        def _():
+            merge(g - 1)
+            final_copy(g - 1).start()
+
         return carry
 
-    def second(g, carry):
-        for i, (top, acc) in enumerate(partials(half // pack + g)):
-            j = g * pack + i
-            pair_copy(j).wait_recv()
-            turned = jnp.transpose(mid[j, rows:, :])
-            best = jnp.maximum(top, turned[:, 0:1])
-            here = jnp.exp2((top - best) * factor)
-            there = jnp.exp2((turned[:, 0:1] - best) * factor)
-            put(
-                half + j,
-                best,
-                acc[:, width:] * here + turned[:, 1:2] * there,
-                acc[:, :width] * here + mid[j, :rows, :] * there,
-            )
-
-            @pl.when(j < half - 1)
-            def _():
-                final_copy(j).start()
-
-        return carry
-
-    lax.fori_loop(0, half // pack, first, 0)
-    lax.fori_loop(0, half // pack, second, 0)
+    lax.fori_loop(0, half - 1, step, 0)
+    top, acc = top_buf[...], None
+    for at in range(0, span, DEPTH):
+        acc = weigh(top, acc, at)
+        if at == span - 2 * DEPTH:
+            merge(half - 2)
+            final_copy(half - 2).start()
+    ship(half - 1, top, acc)
+    merge(half - 1)
 
     for copy in kv + qs + ls + forwards:
         copy.wait_send()
@@ -240,6 +266,7 @@
             pltpu.VMEM((count, req, 128), jnp.int32),
             pltpu.VMEM((req, 128), jnp.int32),
             pltpu.VMEM((big, span), jnp.float32),
+            pltpu.VMEM((big, 128), jnp.float32),
             pltpu.VMEM((count, rows + 8, width), jnp.float32),
             pltpu.VMEM((count // 2, rows + 8, width), jnp.float32),
             pltpu.VMEM((count // 2, rows + 8, width), jnp.float32),

time: 31.7 us -> 32.3 us (1.019)
  Pallas kernels: 29.5 us -> 30.1 us
    pallas_call x1, Pallas kernels: 29.5 us -> 30.1 us  [per_device(): pl.pallas_call(functools.partial(kernel, count, heads, pack), out_shape=j...]
where the time goes in v3:
time: 32.3 us; the launch traced here: 32.1 us
  Pallas kernels  30.1 us (93%)
  local copies, waits for them, and re-layouts  1.38 us (4%)
  between operations  0.66 us (2%)
    pallas_call x1, Pallas kernels, per_device(): pl.pallas_call(functools.partial(kernel, count, heads, pack), out_shape=j...  30.1 us
    unnamed x1, local copies, waits for them, and re-layouts  1.38 us

profile of v3, /device:TPU:0, one launch (start us, length us, event | category | flops | bytes accessed | tf_op | source)
XLA Modules:
  0.0 32.1 jit_solution(3663333383053487339)
XLA Ops:
  0.7 30.1 %shard_map.46 = bf16[128,128]{1,0:T(8,128)(2,1)} custom-call(bf16[128,128]{1,0:T(8,128)(2,1)} %bitcast.3, bf16[1,2,4096,128]{3,2,1,0:T(8,128)(2,1)} %cache_ref.1, s32[1]{0:T(128)S(6)} %copy.6.owner_hbm, s32[8]{0:T(128)} %len_hbm.1), custom_call_target="tpu_custom_call" | custom-call | tf_op jit(solution)/shard_map/pallas_call | solution.py:255
  30.8 1.4 %copy.7 = bf16[8,16,128]{2,1,0:T(8,128)(2,1)} copy(bf16[8,16,128]{2,1,0:T(8,128)(2,1)} %bitcast.2) | data formatting | bytes 65536

commit v4 on v3

--- a/solution.py
+++ b/solution.py
@@ -15,6 +15,14 @@
 
 def distance(slot, count):
     return count // 2 + (1 - 2 * (slot % 2)) * ((slot + 1) // 2)
+
+
+def across(i):
+    return 2 * i - 1 + 1 // (i + 1)
+
+
+def along(i, half):
+    return min(2 * i + 2, 2 * half - 1) if isinstance(i, int) else 2 * i + 2
 
 
 def kernel(
@@ -74,7 +82,7 @@
     qs, forwards, ls = [], [], []
     for i in range(half):
         d = distance(i, half)
-        targets = [(2 * i, 1 - inner), (2 * i + 1, inner)]
+        targets = [(across(i), 1 - inner), (along(i, half), inner)]
         for j, parity in targets if i < half - 1 else targets[:1]:
             ls.append(pltpu.make_async_remote_copy(
                 src_ref=len_out, dst_ref=len_buf.at[j],
@@ -83,13 +91,13 @@
             ))
         if i < half - 1:
             qs.append(pltpu.make_async_remote_copy(
-                src_ref=q_ref, dst_ref=q_buf.at[2 * i + 1],
-                send_sem=q_send.at[2 * i + 1], recv_sem=q_recv.at[2 * i + 1],
+                src_ref=q_ref, dst_ref=q_buf.at[along(i, half)],
+                send_sem=q_send.at[along(i, half)], recv_sem=q_recv.at[along(i, half)],
                 device_id={"ctx": shifted(-d, inner)}, device_id_type=MESH,
             ))
         forwards.append(pltpu.make_async_remote_copy(
-            src_ref=q_buf.at[2 * i + 1], dst_ref=q_buf.at[2 * i],
-            send_sem=q_send.at[2 * i], recv_sem=q_recv.at[2 * i],
+            src_ref=q_buf.at[along(i, half)], dst_ref=q_buf.at[across(i)],
+            send_sem=q_send.at[across(i)], recv_sem=q_recv.at[across(i)],
             device_id={"ctx": beside}, device_id_type=MESH,
         ))
     for copy in qs + ls + forwards[half - 1 :] + kv:
@@ -110,15 +118,15 @@
 
     def pair_copy(i):
         return pltpu.make_async_remote_copy(
-            src_ref=snd.at[2 * i], dst_ref=mid.at[i],
-            send_sem=o_send.at[2 * i], recv_sem=o_recv.at[2 * i],
+            src_ref=snd.at[across(i)], dst_ref=mid.at[i],
+            send_sem=o_send.at[i], recv_sem=o_recv.at[i],
             device_id={"ctx": beside}, device_id_type=MESH,
         )
 
     def final_copy(i):
-        j = 2 * i + 1
+        j = along(i, half)
         return pltpu.make_async_remote_copy(
-            src_ref=snd.at[j], dst_ref=rcv.at[i], send_sem=o_send.at[j], recv_sem=o_recv.at[j],
+            src_ref=snd.at[j], dst_ref=rcv.at[i], send_sem=o_send.at[half + i], recv_sem=o_recv.at[half + i],
             device_id={"ctx": shifted(distance(i, half), inner)}, device_id_type=MESH,
         )
 
@@ -165,24 +173,23 @@
         snd[j, :rows, :] = value
         snd[j, rows:, :] = jnp.transpose(jnp.where(first_lane, top, total))[:8]
 
-    def ship(g, top, acc):
-        for i in range(pack):
-            at = slice(i * rows, (i + 1) * rows)
-            put(g * pack + i, top[at], acc[at, width:], acc[at, :width])
-            if i == 0:
-                pair_copy(g).start()
-
-    def merge(g):
-        j = 2 * g + 1
-        pair_copy(g).wait_recv()
-        mine_ = jnp.transpose(snd[j, rows:, :])
-        theirs_ = jnp.transpose(mid[g, rows:, :])
-        best = jnp.maximum(mine_[:, 0:1], theirs_[:, 0:1])
-        here = jnp.exp2((mine_[:, 0:1] - best) * factor)
-        there = jnp.exp2((theirs_[:, 0:1] - best) * factor)
+    def rows_of(i, top, acc):
+        at = slice(i * rows, (i + 1) * rows)
+        return top[at], acc[at, width:], acc[at, :width]
+
+    def cross(i, top, total, value):
+        put(across(i), top, total, value)
+        pair_copy(i).start()
+
+    def merge(i, top, total, value):
+        pair_copy(i).wait_recv()
+        turned = jnp.transpose(mid[i, rows:, :])
+        best = jnp.maximum(top, turned[:, 0:1])
+        here = jnp.exp2((top - best) * factor)
+        there = jnp.exp2((turned[:, 0:1] - best) * factor)
         put(
-            j, best, mine_[:, 1:2] * here + theirs_[:, 1:2] * there,
-            snd[j, :rows, :] * here + mid[g, :rows, :] * there,
+            along(i, half), best, total * here + turned[:, 1:2] * there,
+            value * here + mid[i, :rows, :] * there,
         )
 
     floor = jnp.full((big, 128), -1e30, jnp.float32)
@@ -191,31 +198,32 @@
     kv[1].wait_recv()
     v_buf[:, :width] = own_kv[1] * mine + got_kv[1] * theirs
 
-    def step(g, carry):
+    def both(g):
         top, acc, later = top_buf[...], None, floor
         q, left = scoring(g + 1)
         for at in range(0, span, DEPTH):
             acc = weigh(top, acc, at)
             later = score(q, left, later, at, at + DEPTH)
         top_buf[...] = spread(later)
-        ship(g, top, acc)
-
-        @pl.when(g > 0)
-        def _():
-            merge(g - 1)
-            final_copy(g - 1).start()
-
+        return top, acc
+
+    def step(g, carry):
+        top, acc = both(g)
+        cross(g + 1, *rows_of(1, top, acc))
+        merge(g - 1, *rows_of(0, top, acc))
+        final_copy(g - 1).start()
         return carry
 
-    lax.fori_loop(0, half - 1, step, 0)
+    top, acc = both(0)
+    cross(0, *rows_of(0, top, acc))
+    cross(1, *rows_of(1, top, acc))
+    lax.fori_loop(1, half - 1, step, 0)
     top, acc = top_buf[...], None
     for at in range(0, span, DEPTH):
         acc = weigh(top, acc, at)
-        if at == span - 2 * DEPTH:
-            merge(half - 2)
-            final_copy(half - 2).start()
-    ship(half - 1, top, acc)
-    merge(half - 1)
+    merge(half - 2, *rows_of(0, top, acc))
+    final_copy(half - 2).start()
+    merge(half - 1, *rows_of(1, top, acc))
 
     for copy in kv + qs + ls + forwards:
         copy.wait_send()

time: 32.3 us -> 30.8 us (0.954)
  Pallas kernels: 30.1 us -> 28.5 us
    pallas_call x1, Pallas kernels: 30.1 us -> 28.5 us  [per_device(): pl.pallas_call(functools.partial(kernel, count, heads, pack), out_shape=j...]
where the time goes in v4:
time: 30.8 us; the launch traced here: 30.6 us
  Pallas kernels  28.5 us (93%)
  local copies, waits for them, and re-layouts  1.38 us (4%)
  between operations  0.66 us (2%)
    pallas_call x1, Pallas kernels, per_device(): pl.pallas_call(functools.partial(kernel, count, heads, pack), out_shape=j...  28.5 us
    unnamed x1, local copies, waits for them, and re-layouts  1.38 us

profile of v4, /device:TPU:0, one launch (start us, length us, event | category | flops | bytes accessed | tf_op | source)
XLA Modules:
  0.0 30.6 jit_solution(8967523740120105684)
XLA Ops:
  0.7 28.5 %shard_map.46 = bf16[128,128]{1,0:T(8,128)(2,1)} custom-call(bf16[128,128]{1,0:T(8,128)(2,1)} %bitcast.3, bf16[1,2,4096,128]{3,2,1,0:T(8,128)(2,1)} %cache_ref.1, s32[1]{0:T(128)S(6)} %copy.6.owner_hbm, s32[8]{0:T(128)} %len_hbm.1), custom_call_target="tpu_custom_call" | custom-call | tf_op jit(solution)/shard_map/pallas_call | solution.py:263
  29.2 1.4 %copy.7 = bf16[8,16,128]{2,1,0:T(8,128)(2,1)} copy(bf16[8,16,128]{2,1,0:T(8,128)(2,1)} %bitcast.2) | data formatting | bytes 65536

commit v5 on v4

--- a/solution.py
+++ b/solution.py
@@ -113,7 +113,7 @@
     locals_[0].wait()
     kv[0].wait_recv()
     k_buf[...] = own_kv[0] * mine + got_kv[0] * theirs
-    for copy in forwards + ls:
+    for copy in forwards[:2] + [ls[0], ls[2]]:
         copy.wait_recv()
 
     def pair_copy(i):
@@ -155,10 +155,10 @@
                 top = jnp.maximum(top, part)
         return top
 
-    def weigh(top, acc, at):
+    def weigh(top, acc, at, begin=0, end=big):
         w = jnp.concatenate(
             [
-                jnp.exp2((s_buf[:, i : i + 128] - top) * factor).astype(jnp.bfloat16)
+                jnp.exp2((s_buf[begin:end, i : i + 128] - top) * factor).astype(jnp.bfloat16)
                 for i in range(at, at + DEPTH, 128)
             ],
             axis=1,
@@ -194,6 +194,8 @@
 
     floor = jnp.full((big, 128), -1e30, jnp.float32)
     top_buf[...] = spread(score(*scoring(0), floor, 0, span))
+    for copy in forwards[2:] + ls[1:2] + ls[3:]:
+        copy.wait_recv()
     locals_[1].wait()
     kv[1].wait_recv()
     v_buf[:, :width] = own_kv[1] * mine + got_kv[1] * theirs
@@ -218,12 +220,14 @@
     cross(0, *rows_of(0, top, acc))
     cross(1, *rows_of(1, top, acc))
     lax.fori_loop(1, half - 1, step, 0)
-    top, acc = top_buf[...], None
-    for at in range(0, span, DEPTH):
-        acc = weigh(top, acc, at)
-    merge(half - 2, *rows_of(0, top, acc))
-    final_copy(half - 2).start()
-    merge(half - 1, *rows_of(1, top, acc))
+    for i in range(pack):
+        begin, end = i * rows, (i + 1) * rows
+        top, acc = top_buf[begin:end, :], None
+        for at in range(0, span, DEPTH):
+            acc = weigh(top, acc, at, begin, end)
+        merge(half - pack + i, top, acc[:, width:], acc[:, :width])
+        if i == 0:
+            final_copy(half - 2).start()
 
     for copy in kv + qs + ls + forwards:
         copy.wait_send()

time: 30.8 us -> 30.7 us (level)
  no operation moved by 1% of the time
where the time goes in v5:
time: 30.7 us; the launch traced here: 30.5 us
  Pallas kernels  28.5 us (93%)
  local copies, waits for them, and re-layouts  1.38 us (4%)
  between operations  0.66 us (2%)
    pallas_call x1, Pallas kernels, per_device(): pl.pallas_call(functools.partial(kernel, count, heads, pack), out_shape=j...  28.5 us
    unnamed x1, local copies, waits for them, and re-layouts  1.38 us

profile of v5, /device:TPU:0, one launch (start us, length us, event | category | flops | bytes accessed | tf_op | source)
XLA Modules:
  0.0 30.5 jit_solution(16394004723415077499)
XLA Ops:
  0.7 28.5 %shard_map.46 = bf16[128,128]{1,0:T(8,128)(2,1)} custom-call(bf16[128,128]{1,0:T(8,128)(2,1)} %bitcast.3, bf16[1,2,4096,128]{3,2,1,0:T(8,128)(2,1)} %cache_ref.1, s32[1]{0:T(128)S(6)} %copy.6.owner_hbm, s32[8]{0:T(128)} %len_hbm.1), custom_call_target="tpu_custom_call" | custom-call | tf_op jit(solution)/shard_map/pallas_call | solution.py:267
  29.2 1.4 %copy.7 = bf16[8,16,128]{2,1,0:T(8,128)(2,1)} copy(bf16[8,16,128]{2,1,0:T(8,128)(2,1)} %bitcast.2) | data formatting | bytes 65536
